TPU v7x, 256 devices: a whole 4x4x8 slice. The times are simulated.
256 devices in a mesh: leaf: 32 (over z, y), front: 8 (over x, core).
Axes of the slice: x: 4, y: 4, z: 8, core: 2. Of those that a mesh axis runs over, the one named last changes fastest.
Arguments:
- leaf_fronts: float32 [32, 1024, 1024], P('leaf', 'front')
- coupling_cols: int32 [32, 8, 124, 128], P('leaf', 'front'), may hold values from 0 to 1023, as said below
- coupling_vals: float32 [32, 8, 124, 128], P('leaf', 'front'), may hold values from -0.1 to 0.1
- sep_diag: float32 [32, 8, 124], P('leaf', 'front'), may hold values from 1 to 3
- child_maps: int32 [62, 512], replicated, may hold values from 0 to 1023, as said below
Outputs:
- factors: float32 [32, 8, 252, 512], P('leaf', 'front')
- log_det: float32 [], replicated
Inputs may be any that keep to these rules, and one draw needn't show every extreme that they name: `coupling_cols`: each coupling column is at most the index, in its front, of the row that holds it, so every entry lies on or below the diagonal. `child_maps`: the 512 entries of each row are distinct.
All inputs are finite; a program needn't handle non-finite values.
Results may differ from a plain program's by a relative error of at most 0.0001.
Values sent between devices are 32-bit elements; how exact they have to be, the bound alone decides.
A program may use at most 128 MiB of HBM per device.

v0:
```python
import jax
import jax.numpy as jnp
from jax import lax
from jax.sharding import PartitionSpec as P

SEP = 512
BND = 512
highest_precision = lax.Precision.HIGHEST


def swapped(block, axis, distance):
    count = lax.axis_size(axis)
    route = []
    for low in range(count):
        high = low | 1 << distance
        if high != low and high < count:
            route += [(low, high), (high, low)]
    return lax.ppermute(block, axis, route)


def from_behind(block, axis, distance):
    devices = range(lax.axis_size(axis))
    route = [(i - distance, i) for i in devices if i - distance in devices]
    return lax.ppermute(block, axis, route)


def symmetric_of(lower_tri):
    return lower_tri + lower_tri.T - jnp.diag(jnp.diag(lower_tri))


def double_up(gathered, partner, bit_pos):
    leaf_pos = lax.axis_index("leaf")
    high_side = leaf_pos >> bit_pos & 1 == 1
    first_half = jnp.where(high_side, partner, gathered)
    second_half = jnp.where(high_side, gathered, partner)
    return jnp.concatenate([first_half, second_half], axis=0)


def collect(strip_piece, bit_count, is_panel):
    if is_panel:
        gathered = lax.all_gather(strip_piece, "front", axis=0, tiled=True)
    else:
        gathered = lax.all_gather(strip_piece, "front", axis=0, tiled=True)
    for bit_pos in range(bit_count):
        if is_panel:
            partner = swapped(gathered, "leaf", bit_pos)
        else:
            partner = swapped(gathered, "leaf", bit_pos)
        gathered = double_up(gathered, partner, bit_pos)
    return gathered


def twin_order(gathered, group_size):
    row_count = gathered.shape[0] // (2 * group_size)
    col_count = gathered.shape[1]
    arranged = gathered.reshape(2, 2, group_size // 2, row_count, col_count)
    return arranged.transpose(0, 2, 1, 3, 4).reshape(2, group_size * row_count, col_count)


def child_rows(update_rows, index_map, row_ids):
    match_grid = index_map[None, :] == row_ids[:, None]
    child_ids = jnp.arange(index_map.shape[0], dtype=jnp.int32)
    present = jnp.any(match_grid, axis=1)
    source = jnp.sum(jnp.where(match_grid, child_ids[None, :], 0), axis=1)
    row_part = jnp.take(update_rows, source, axis=0)
    col_part = jnp.take(update_rows, source, axis=1).T
    picked = jnp.where(child_ids[None, :] <= source[:, None], row_part, col_part)
    return jnp.where(present[:, None], picked, 0.0)


def body(leaf_fronts, coupling_cols, coupling_vals, sep_diag, child_maps):
    group_count = lax.axis_size("leaf")
    front_count = lax.axis_size("front")
    level_total = group_count.bit_length()
    width_all = SEP + BND
    leaf_pos = lax.axis_index("leaf")
    front_pos = lax.axis_index("front")
    size_rows = width_all // front_count
    row_ids = front_pos * size_rows + jnp.arange(size_rows, dtype=jnp.int32)
    column_ids = jnp.arange(width_all, dtype=jnp.int32)
    front_strip = jnp.where(column_ids[None, :] <= row_ids[:, None], leaf_fronts[0], 0.0)
    pieces_out = []
    log_part = jnp.zeros((), jnp.float32)
    list_offset = 0
    map_base = 0
    for level_no in range(level_total):
        span_leaf = 1 << level_no
        size_rows = width_all // (front_count * span_leaf)
        group_rank = (leaf_pos & span_leaf - 1) * front_count + front_pos
        start_row = group_rank * size_rows
        panel_piece = front_strip[:, :SEP]
        panel_cols = collect(panel_piece, level_no, True)
        head_block = symmetric_of(panel_cols[:SEP])
        chol_head = jnp.linalg.cholesky(head_block)
        below = jax.scipy.linalg.solve_triangular(chol_head, panel_cols[SEP:].T, lower=True).T
        factor_cols = jnp.concatenate([chol_head, below], axis=0)
        pieces_out.append(lax.dynamic_slice_in_dim(factor_cols, start_row, size_rows, 0))
        head_diag = jnp.diagonal(chol_head)
        owned_rows = jnp.arange(SEP, dtype=jnp.int32) // size_rows == group_rank
        log_part = log_part + jnp.sum(jnp.where(owned_rows, jnp.log(head_diag), 0.0))
        if level_no + 1 < level_total:
            group_size = span_leaf * front_count
            half_rows = size_rows // 2
            holds_tail = group_rank >= group_size // 2
            update_start = start_row - jnp.where(holds_tail, SEP, 0)
            tail_rows = front_strip[:, SEP:]

            def tail_term():
                own_below = lax.dynamic_slice_in_dim(
                    below, jnp.clip(update_start, 0, BND - size_rows), size_rows, 0
                )
                return tail_rows - jnp.dot(
                    own_below,
                    below.T,
                    precision=highest_precision,
                    preferred_element_type=jnp.float32,
                )

            def empty_term():
                return jnp.zeros((size_rows, BND), jnp.float32)

            difference = lax.cond(holds_tail, tail_term, empty_term)
            leading = difference[:half_rows]
            if level_no == 0:
                received = from_behind(leading, "front", -(front_count // 2))
            else:
                received = from_behind(leading, "leaf", -(1 << level_no - 1))
            outgoing = jnp.where(holds_tail, difference[half_rows:], received)
            gathered = twin_order(collect(outgoing, level_no + 1, False), group_size)
            parent_span = span_leaf * 2
            next_rows = width_all // (front_count * parent_span)
            parent_rank = (leaf_pos & parent_span - 1) * front_count + front_pos
            row_ids = parent_rank * next_rows + jnp.arange(next_rows, dtype=jnp.int32)
            parent_no = leaf_pos >> level_no + 1
            assembled = jnp.zeros((next_rows, width_all), jnp.float32)
            for child_no in range(2):
                index_map = lax.dynamic_slice_in_dim(
                    child_maps, map_base + 2 * parent_no + child_no, 1, 0
                )[0]
                picked = child_rows(gathered[child_no], index_map, row_ids)
                assembled = assembled.at[:, index_map].add(picked)
            assembled = jnp.where(column_ids[None, :] <= row_ids[:, None], assembled, 0.0)
            col_block = coupling_cols[0, 0, list_offset : list_offset + next_rows, :]
            val_block = coupling_vals[0, 0, list_offset : list_offset + next_rows, :]
            local_rows = jnp.arange(next_rows, dtype=jnp.int32)
            assembled = assembled.at[local_rows[:, None], col_block].add(val_block)
            diag_piece = sep_diag[0, 0, list_offset : list_offset + next_rows]
            assembled = assembled + jnp.where(
                column_ids[None, :] == row_ids[:, None], diag_piece[:, None], 0.0
            )
            front_strip = assembled
            list_offset = list_offset + next_rows
            map_base = map_base + group_count // span_leaf
    log_det = 2.0 * lax.psum(log_part, ("leaf", "front"))
    factors = jnp.concatenate(pieces_out, axis=0)[None, None]
    return (factors, log_det)


def solution(mesh):
    placed = (
        P("leaf", "front", None),
        P("leaf", "front", None, None),
        P("leaf", "front", None, None),
        P("leaf", "front", None),
        P(),
    )
    return jax.shard_map(
        body,
        mesh=mesh,
        in_specs=placed,
        out_specs=(P("leaf", "front", None, None), P()),
        check_vma=False,
    )
```

profile of v0, /device:TPU:1, one launch (start us, length us, event | category | flops | bytes accessed | tf_op | source)
XLA Modules:
  0.0 2185.0 jit_solution(17562657626396560996)
XLA Ops:
  9.3 33.1 %all-gather.6.cloned.1.call-done = f32[1024,512]{1,0:T(8,128)} async-done(((f32[128,512]{1,0:T(8,128)}), f32[1024,512]{1,0:T(8,128)}) %all-gather.6.cloned.1.call-update) | async-done | bytes 2097168 | tf_op jit(solution)/shard_map/all_gather | solution.py:41
  152.5 39.3 %custom-call.72 = f32[4,128,128]{1,2,0:T(8,128)S(1)} custom-call(f32[4,128,128]{2,1,0:T(8,128)S(1)} %get-tuple-element.167), custom_call_target="InvertDiagBlocksLowerTriangular" | custom-call | tf_op jit(solution)/shard_map/jit(_solve_triangular)/triangular_solve | solution.py:95
  215.7 23.5 %all-gather.8.cloned.1.call-done = f32[512,512]{1,0:T(8,128)} async-done(((f32[64,512]{1,0:T(8,128)}), f32[512,512]{1,0:T(8,128)}) %all-gather.8.cloned.1.call-update) | async-done | bytes 1048592 | tf_op jit(solution)/shard_map/all_gather | solution.py:43
  243.6 20.4 collective-permute-done.1
  278.8 57.0 %scatter_fusion.6 = f32[65536]{0:T(1024)S(1)} fusion(f32[65536]{0:T(1024)S(1)} %bitcast.497, s32[8192]{0:T(1024)S(1)} %copy-done.34, f32[8192]{0:T(1024)S(1)} %bitcast.526), kind=kCustom, calls=%fused_computation.43 | custom fusion | flops 8192 | bytes 131072
  336.7 26.7 %all-gather.10.cloned.1.call-done = f32[512,512]{1,0:T(8,128)} async-done(((f32[64,512]{1,0:T(8,128)}), f32[512,512]{1,0:T(8,128)}) %all-gather.10.cloned.1.call-update) | async-done | bytes 1048592 | tf_op jit(solution)/shard_map/all_gather | solution.py:41
  365.8 22.4 %collective-permute-done.2 = f32[512,512]{1,0:T(8,128)S(1)} collective-permute-done((f32[512,512]{1,0:T(8,128)}, f32[512,512]{1,0:T(8,128)S(1)}, u32[]{:S(2)}, u32[]{:S(2)}) %collective-permute-start.2) | collective-permute-done | bytes 1048608 | tf_op jit(solution)/shard_map/ppermute | solution.py:18
  500.6 39.9 %custom-call.76 = f32[4,128,128]{1,2,0:T(8,128)} custom-call(f32[4,128,128]{2,1,0:T(8,128)S(1)} %get-tuple-element.168), custom_call_target="InvertDiagBlocksLowerTriangular" | custom-call | tf_op jit(solution)/shard_map/jit(_solve_triangular)/triangular_solve | solution.py:95
  567.6 14.9 all_gather.36
  602.7 22.6 %collective-permute-done.5 = f32[512,512]{1,0:T(8,128)} collective-permute-done((f32[512,512]{1,0:T(8,128)}, f32[512,512]{1,0:T(8,128)}, u32[]{:S(2)}, u32[]{:S(2)}) %collective-permute-start.5) | collective-permute-done | bytes 1048608 | tf_op jit(solution)/shard_map/ppermute | solution.py:18
  647.6 28.8 %scatter_fusion.7 = f32[32768]{0:T(1024)S(1)} fusion(f32[32768]{0:T(1024)S(1)} %bitcast.498, s32[4096]{0:T(1024)S(1)} %select_bitcast_fusion.24, f32[4096]{0:T(1024)S(1)} %bitcast.527), kind=kCustom, calls=%fused_computation.44 | custom fusion | flops 4096 | bytes 65536
  676.5 14.3 all_gather.37
  708.2 22.3 %collective-permute-done.7 = f32[512,512]{1,0:T(8,128)} collective-permute-done((f32[512,512]{1,0:T(8,128)S(1)}, f32[512,512]{1,0:T(8,128)}, u32[]{:S(2)}, u32[]{:S(2)}) %collective-permute-start.7) | collective-permute-done | bytes 1048608 | tf_op jit(solution)/shard_map/ppermute | solution.py:18
  851.2 39.9 %custom-call.80 = f32[4,128,128]{1,2,0:T(8,128)} custom-call(f32[4,128,128]{2,1,0:T(8,128)S(1)} %get-tuple-element.169), custom_call_target="InvertDiagBlocksLowerTriangular" | custom-call | tf_op jit(solution)/shard_map/jit(_solve_triangular)/triangular_solve | solution.py:95
  919.4 15.4 all_gather.38
  961.3 21.7 collective-permute-done.11
  1005.2 14.7 scatter_fusion.8
  1019.9 15.2 all_gather.39
  1059.3 21.6 collective-permute-done.14
  1198.1 39.9 %custom-call.84 = f32[4,128,128]{1,2,0:T(8,128)} custom-call(f32[4,128,128]{2,1,0:T(8,128)S(1)} %get-tuple-element.170), custom_call_target="InvertDiagBlocksLowerTriangular" | custom-call | tf_op jit(solution)/shard_map/jit(_solve_triangular)/triangular_solve | solution.py:95
  1264.3 16.2 all_gather.40
  1314.1 45.0 %collective-permute-done.19 = f32[512,512]{1,0:T(8,128)} collective-permute-done((f32[512,512]{1,0:T(8,128)}, f32[512,512]{1,0:T(8,128)}, u32[]{:S(2)}, u32[]{:S(2)}) %collective-permute-start.19) | collective-permute-done | bytes 1048608 | tf_op jit(solution)/shard_map/ppermute | solution.py:18
  1431.5 45.2 %collective-permute-done.23 = f32[512,512]{1,0:T(8,128)} collective-permute-done((f32[512,512]{1,0:T(8,128)S(1)}, f32[512,512]{1,0:T(8,128)}, u32[]{:S(2)}, u32[]{:S(2)}) %collective-permute-start.23) | collective-permute-done | bytes 1048608 | tf_op jit(solution)/shard_map/ppermute | solution.py:18
  1594.0 39.9 %custom-call.88 = f32[4,128,128]{1,2,0:T(8,128)} custom-call(f32[4,128,128]{2,1,0:T(8,128)S(1)} %get-tuple-element.171), custom_call_target="InvertDiagBlocksLowerTriangular" | custom-call | tf_op jit(solution)/shard_map/jit(_solve_triangular)/triangular_solve | solution.py:95
  1659.4 15.1 all-gather
  1695.8 22.6 %collective-permute-done.28 = f32[256,512]{1,0:T(8,128)} collective-permute-done((f32[256,512]{1,0:T(8,128)S(1)}, f32[256,512]{1,0:T(8,128)}, u32[]{:S(2)}, u32[]{:S(2)}) %collective-permute-start.28) | collective-permute-done | bytes 524320 | tf_op jit(solution)/shard_map/ppermute | solution.py:18
  1722.7 47.7 %collective-permute-done.29 = f32[512,512]{1,0:T(8,128)} collective-permute-done((f32[512,512]{1,0:T(8,128)}, f32[512,512]{1,0:T(8,128)}, u32[]{:S(2)}, u32[]{:S(2)}) %collective-permute-start.29) | collective-permute-done | bytes 1048608 | tf_op jit(solution)/shard_map/ppermute | solution.py:18
  1801.1 24.8 %scatter_fusion.5 = f32[4,1024]{1,0:T(4,128)S(1)} fusion(f32[4,1024]{1,0:T(4,128)S(1)} %add.625, s32[512]{0:T(512)S(1)} %fusion.262, f32[512]{0:T(512)S(1)} %bitcast.530), kind=kCustom, calls=%fused_computation.42 | custom fusion | flops 512 | bytes 10240 | tf_op jit(solution)/shard_map/scatter-add | solution.py:146
  1861.9 18.8 collective-permute-done.33
  1913.9 20.8 collective-permute-done.34
  2040.2 39.3 %custom-call.92 = f32[4,128,128]{1,2,0:T(8,128)S(1)} custom-call(f32[4,128,128]{2,1,0:T(8,128)S(1)} %get-tuple-element.172), custom_call_target="InvertDiagBlocksLowerTriangular" | custom-call | tf_op jit(solution)/shard_map/jit(_solve_triangular)/triangular_solve | solution.py:95
  2095.1 76.0 %psum.7 = f32[]{:T(128)} all-reduce(f32[]{:T(128)S(6)} %add.634), channel_id=1, replica_groups=mesh['leaf'=32,'front'=8] {'leaf','front'}, use_global_device_ids=true, to_apply=%region_59.72 | all-reduce | flops 1 | bytes 8 | tf_op jit(solution)/shard_map/psum | solution.py:154
  (823 shorter events, 1270.8 us)
Async XLA Ops:
  7.2 35.2 %all-gather.6.cloned.1.call-start = ((), (), s32[]{:S(2)}) async-start(), calls=%async_computation | async-start | bytes 2359296 | tf_op jit(solution)/shard_map/all_gather | solution.py:41
  9.2 230.0 %all-gather.8.cloned.1.call-start = ((), (), s32[]{:S(2)}) async-start(), calls=%async_computation.1 | async-start | bytes 1179648 | tf_op jit(solution)/shard_map/all_gather | solution.py:43
  204.3 8.8 collective-permute-start
  213.7 149.7 %all-gather.10.cloned.1.call-start = ((), (), s32[]{:S(2)}) async-start(), calls=%async_computation.2 | async-start | bytes 1179648 | tf_op jit(solution)/shard_map/all_gather | solution.py:41
  239.2 24.7 %collective-permute-start.1 = (f32[512,512]{1,0:T(8,128)}, f32[512,512]{1,0:T(8,128)S(1)}, u32[]{:S(2)}, u32[]{:S(2)}) collective-permute-start(f32[512,512]{1,0:T(8,128)} %all-gather.8.cloned.1.call-done), channel_id=1, source_target_pairs={{0,8},{8,0},{16,24},{24,16},{32,40},{40,32},{48,56},{56,48},{64,72... | collective-permute-start | bytes 3145736 | tf_op jit(solution)/shard_map/ppermute | solution.py:18
  363.4 24.7 %collective-permute-start.2 = (f32[512,512]{1,0:T(8,128)}, f32[512,512]{1,0:T(8,128)S(1)}, u32[]{:S(2)}, u32[]{:S(2)}) collective-permute-start(f32[512,512]{1,0:T(8,128)} %all-gather.10.cloned.1.call-done), channel_id=1, source_target_pairs={{0,8},{8,0},{16,24},{24,16},{32,40},{40,32},{48,56},{56,48},{64,72... | collective-permute-start | bytes 3145736 | tf_op jit(solution)/shard_map/ppermute | solution.py:18
  560.8 6.8 collective-permute-start.3
  582.4 14.0 collective-permute-start.4
  597.6 27.7 %collective-permute-start.5 = (f32[512,512]{1,0:T(8,128)}, f32[512,512]{1,0:T(8,128)}, u32[]{:S(2)}, u32[]{:S(2)}) collective-permute-start(f32[512,512]{1,0:T(8,128)} %pad_maximum_fusion.7), channel_id=1, source_target_pairs={{0,16},{16,0},{8,24},{24,8},{32,48},{48,32},{40,56},{56,40},{64,80... | collective-permute-start | bytes 3145736 | tf_op jit(solution)/shard_map/ppermute | solution.py:18
  690.8 13.4 collective-permute-start.6
  705.2 25.3 %collective-permute-start.7 = (f32[512,512]{1,0:T(8,128)S(1)}, f32[512,512]{1,0:T(8,128)}, u32[]{:S(2)}, u32[]{:S(2)}) collective-permute-start(f32[512,512]{1,0:T(8,128)S(1)} %pad_maximum_fusion.8), channel_id=1, source_target_pairs={{0,16},{16,0},{8,24},{24,8},{32,48},{48,32},{40,56},{56,40},{64,80... | collective-permute-start | bytes 3145736 | tf_op jit(solution)/shard_map/ppermute | solution.py:18
  911.3 8.1 collective-permute-start.8
  934.8 7.8 collective-permute-start.9
  942.7 15.5 collective-permute-start.10
  959.4 23.6 %collective-permute-start.11 = (f32[512,512]{1,0:T(8,128)}, f32[512,512]{1,0:T(8,128)}, u32[]{:S(2)}, u32[]{:S(2)}) collective-permute-start(f32[512,512]{1,0:T(8,128)} %pad_maximum_fusion.10), channel_id=1, source_target_pairs={{0,32},{32,0},{8,40},{40,8},{16,48},{48,16},{24,56},{56,24},{64,96... | collective-permute-start | bytes 3145736 | tf_op jit(solution)/shard_map/ppermute | solution.py:18
  1035.1 7.8 collective-permute-start.12
  1042.9 14.0 collective-permute-start.13
  1058.1 22.9 %collective-permute-start.14 = (f32[512,512]{1,0:T(8,128)S(1)}, f32[512,512]{1,0:T(8,128)}, u32[]{:S(2)}, u32[]{:S(2)}) collective-permute-start(f32[512,512]{1,0:T(8,128)S(1)} %pad_maximum_fusion.11), channel_id=1, source_target_pairs={{0,32},{32,0},{8,40},{40,8},{16,48},{48,16},{24,56},{56,24},{64,96... | collective-permute-start | bytes 3145736 | tf_op jit(solution)/shard_map/ppermute | solution.py:18
  1258.2 6.1 collective-permute-start.15
  1285.6 8.4 collective-permute-start.17
  1294.1 12.2 collective-permute-start.18
  1307.4 51.7 %collective-permute-start.19 = (f32[512,512]{1,0:T(8,128)}, f32[512,512]{1,0:T(8,128)}, u32[]{:S(2)}, u32[]{:S(2)}) collective-permute-start(f32[512,512]{1,0:T(8,128)} %pad_maximum_fusion.13), channel_id=1, source_target_pairs={{0,64},{64,0},{8,72},{72,8},{16,80},{80,16},{24,88},{88,24},{32,96... | collective-permute-start | bytes 3145736 | tf_op jit(solution)/shard_map/ppermute | solution.py:18
  1407.9 8.4 collective-permute-start.21
  1416.4 11.6 collective-permute-start.22
  1429.1 47.6 %collective-permute-start.23 = (f32[512,512]{1,0:T(8,128)S(1)}, f32[512,512]{1,0:T(8,128)}, u32[]{:S(2)}, u32[]{:S(2)}) collective-permute-start(f32[512,512]{1,0:T(8,128)S(1)} %pad_maximum_fusion.14), channel_id=1, source_target_pairs={{0,64},{64,0},{8,72},{72,8},{16,80},{80,16},{24,88},{88,24},{32,96... | collective-permute-start | bytes 3145736 | tf_op jit(solution)/shard_map/ppermute | solution.py:18
  1678.2 5.4 collective-permute-start.26
  1683.6 7.2 collective-permute-start.27
  1691.6 26.7 %collective-permute-start.28 = (f32[256,512]{1,0:T(8,128)S(1)}, f32[256,512]{1,0:T(8,128)}, u32[]{:S(2)}, u32[]{:S(2)}) collective-permute-start(f32[256,512]{1,0:T(8,128)S(1)} %pad_maximum_fusion.22), channel_id=1, source_target_pairs={{0,64},{64,0},{8,72},{72,8},{16,80},{80,16},{24,88},{88,24},{32,96... | collective-permute-start | bytes 1572872 | tf_op jit(solution)/shard_map/ppermute | solution.py:18
  1720.6 49.7 %collective-permute-start.29 = (f32[512,512]{1,0:T(8,128)}, f32[512,512]{1,0:T(8,128)}, u32[]{:S(2)}, u32[]{:S(2)}) collective-permute-start(f32[512,512]{1,0:T(8,128)} %pad_maximum_fusion.16), channel_id=1, source_target_pairs={{0,128},{128,0},{8,136},{136,8},{16,144},{144,16},{24,152},{152,24... | collective-permute-start | bytes 3145736 | tf_op jit(solution)/shard_map/ppermute | solution.py:18
  1848.7 5.7 collective-permute-start.32
  1855.2 25.5 %collective-permute-start.33 = (f32[256,512]{1,0:T(8,128)S(1)}, f32[256,512]{1,0:T(8,128)}, u32[]{:S(2)}, u32[]{:S(2)}) collective-permute-start(f32[256,512]{1,0:T(8,128)S(1)} %pad_maximum_fusion.23), channel_id=1, source_target_pairs={{0,64},{64,0},{8,72},{72,8},{16,80},{80,16},{24,88},{88,24},{32,96... | collective-permute-start | bytes 1572872 | tf_op jit(solution)/shard_map/ppermute | solution.py:18
  1883.1 51.6 %collective-permute-start.34 = (f32[512,512]{1,0:T(8,128)}, f32[512,512]{1,0:T(8,128)}, u32[]{:S(2)}, u32[]{:S(2)}) collective-permute-start(f32[512,512]{1,0:T(8,128)} %pad_maximum_fusion.17), channel_id=1, source_target_pairs={{0,128},{128,0},{8,136},{136,8},{16,144},{144,16},{24,152},{152,24... | collective-permute-start | bytes 3145736 | tf_op jit(solution)/shard_map/ppermute | solution.py:18
  (82 other events, 1214.8 us)
Sparse Core Ops, SparseCore 0:
  10.4 31.8 all-gather.5
  213.9 25.3 all-gather.7
  336.8 26.5 all-gather.9
where the time goes:
time: 2200 us; the launch traced here: 2180 us
  other arithmetic  971 us (44%)
  waiting for transfers between devices  565 us (26%)
  local copies, waits for them, and re-layouts  249 us (11%)
  blocking collectives  195 us (9%)
  matrix products  98.3 us (4%)
  starting transfers between devices  68.1 us (3%)
  between operations  37.8 us (2%)
    another operation x89, other arithmetic, body(): chol_head = jnp.linalg.cholesky(head_block)  479 us
    ppermute x30, waiting for transfers between devices, swapped(): return lax.ppermute(block, axis, route)  454 us
    another operation x18, other arithmetic, body(): jax.scipy.linalg.solve_triangular(chol_head, panel_cols[SEP:].T, lower=True)  258 us
    all_gather x8, blocking collectives, collect(): gathered = lax.all_gather(strip_piece, 'front', axis=0, tiled=True)  119 us
    unnamed x22, other arithmetic  113 us
    another operation x97, local copies, waits for them, and re-layouts, body(): jax.scipy.linalg.solve_triangular(chol_head, panel_cols[SEP:].T, lower=True)  89.5 us
    all_gather x3, waiting for transfers between devices, collect(): gathered = lax.all_gather(strip_piece, 'front', axis=0, tiled=True)  83.3 us
    psum x1, blocking collectives, body(): log_det = 2.0 * lax.psum(log_part, ('leaf', 'front'))  76 us
  transfers between devices with their start and end apart: 38, of which 38 were waited for; matrix products, arithmetic and copies ran while one was open for 2% of the time, Pallas kernels for 0%

commit v1 on v0

--- a/solution.py
+++ b/solution.py
@@ -2,6 +2,7 @@
 import jax.numpy as jnp
 from jax import lax
 from jax.sharding import PartitionSpec as P
+from jax.lax import psum
 
 SEP = 512
 BND = 512
@@ -151,7 +152,7 @@
             front_strip = assembled
             list_offset = list_offset + next_rows
             map_base = map_base + group_count // span_leaf
-    log_det = 2.0 * lax.psum(log_part, ("leaf", "front"))
+    log_det = 2.0 * psum(psum(log_part, axis_name="front"), axis_name="leaf")
     factors = jnp.concatenate(pieces_out, axis=0)[None, None]
     return (factors, log_det)
 

time: 2200 us -> 2210 us (level)
    psum x1 -> x2, blocking collectives: 76 us -> 74.6 us  [body(): log_det = 2.0 * psum(psum(log_part, axis_name='front'), axis_name='leaf')]
where the time goes in v1:
time: 2210 us; the launch traced here: 2180 us
  other arithmetic  971 us (44%)
  waiting for transfers between devices  565 us (26%)
  local copies, waits for them, and re-layouts  247 us (11%)
  blocking collectives  193 us (9%)
  matrix products  94.7 us (4%)
  starting transfers between devices  68.2 us (3%)
  between operations  37.8 us (2%)
    another operation x89, other arithmetic, body(): chol_head = jnp.linalg.cholesky(head_block)  479 us
    ppermute x30, waiting for transfers between devices, swapped(): return lax.ppermute(block, axis, route)  454 us
    another operation x18, other arithmetic, body(): jax.scipy.linalg.solve_triangular(chol_head, panel_cols[SEP:].T, lower=True)  258 us
    all_gather x8, blocking collectives, collect(): gathered = lax.all_gather(strip_piece, 'front', axis=0, tiled=True)  119 us
    unnamed x22, other arithmetic  113 us
    another operation x97, local copies, waits for them, and re-layouts, body(): jax.scipy.linalg.solve_triangular(chol_head, panel_cols[SEP:].T, lower=True)  89 us
    all_gather x3, waiting for transfers between devices, collect(): gathered = lax.all_gather(strip_piece, 'front', axis=0, tiled=True)  83.3 us
    psum x2, blocking collectives, body(): log_det = 2.0 * psum(psum(log_part, axis_name='front'), axis_name='leaf')  74.6 us
  transfers between devices with their start and end apart: 38, of which 38 were waited for; matrix products, arithmetic and copies ran while one was open for 2% of the time, Pallas kernels for 0%

profile of v1, /device:TPU:1, one launch (start us, length us, event | category | flops | bytes accessed | tf_op | source)
XLA Modules:
  0.0 2177.4 jit_solution(17776904804176566811)
XLA Ops:
  9.3 33.1 %all-gather.6.cloned.1.call-done = f32[1024,512]{1,0:T(8,128)} async-done(((f32[128,512]{1,0:T(8,128)}), f32[1024,512]{1,0:T(8,128)}) %all-gather.6.cloned.1.call-update) | async-done | bytes 2097168 | tf_op jit(solution)/shard_map/all_gather | solution.py:42
  149.4 39.3 %custom-call.72 = f32[4,128,128]{1,2,0:T(8,128)S(1)} custom-call(f32[4,128,128]{2,1,0:T(8,128)S(1)} %get-tuple-element.167), custom_call_target="InvertDiagBlocksLowerTriangular" | custom-call | tf_op jit(solution)/shard_map/jit(_solve_triangular)/triangular_solve | solution.py:96
  212.6 23.5 %all-gather.8.cloned.1.call-done = f32[512,512]{1,0:T(8,128)} async-done(((f32[64,512]{1,0:T(8,128)}), f32[512,512]{1,0:T(8,128)}) %all-gather.8.cloned.1.call-update) | async-done | bytes 1048592 | tf_op jit(solution)/shard_map/all_gather | solution.py:44
  240.5 20.4 collective-permute-done.1
  275.7 57.0 %scatter_fusion.6 = f32[65536]{0:T(1024)S(1)} fusion(f32[65536]{0:T(1024)S(1)} %bitcast.497, s32[8192]{0:T(1024)S(1)} %copy-done.36, f32[8192]{0:T(1024)S(1)} %bitcast.526), kind=kCustom, calls=%fused_computation.43 | custom fusion | flops 8192 | bytes 131072
  333.6 26.7 %all-gather.10.cloned.1.call-done = f32[512,512]{1,0:T(8,128)} async-done(((f32[64,512]{1,0:T(8,128)}), f32[512,512]{1,0:T(8,128)}) %all-gather.10.cloned.1.call-update) | async-done | bytes 1048592 | tf_op jit(solution)/shard_map/all_gather | solution.py:42
  362.7 22.4 %collective-permute-done.2 = f32[512,512]{1,0:T(8,128)S(1)} collective-permute-done((f32[512,512]{1,0:T(8,128)}, f32[512,512]{1,0:T(8,128)S(1)}, u32[]{:S(2)}, u32[]{:S(2)}) %collective-permute-start.2) | collective-permute-done | bytes 1048608 | tf_op jit(solution)/shard_map/ppermute | solution.py:19
  497.5 39.9 %custom-call.76 = f32[4,128,128]{1,2,0:T(8,128)} custom-call(f32[4,128,128]{2,1,0:T(8,128)S(1)} %get-tuple-element.168), custom_call_target="InvertDiagBlocksLowerTriangular" | custom-call | tf_op jit(solution)/shard_map/jit(_solve_triangular)/triangular_solve | solution.py:96
  564.5 14.9 all_gather.36
  599.6 22.6 %collective-permute-done.5 = f32[512,512]{1,0:T(8,128)} collective-permute-done((f32[512,512]{1,0:T(8,128)}, f32[512,512]{1,0:T(8,128)}, u32[]{:S(2)}, u32[]{:S(2)}) %collective-permute-start.5) | collective-permute-done | bytes 1048608 | tf_op jit(solution)/shard_map/ppermute | solution.py:19
  644.5 28.8 %scatter_fusion.7 = f32[32768]{0:T(1024)S(1)} fusion(f32[32768]{0:T(1024)S(1)} %bitcast.498, s32[4096]{0:T(1024)S(1)} %select_bitcast_fusion.24, f32[4096]{0:T(1024)S(1)} %bitcast.527), kind=kCustom, calls=%fused_computation.44 | custom fusion | flops 4096 | bytes 65536
  673.4 14.3 all_gather.37
  705.1 22.3 %collective-permute-done.7 = f32[512,512]{1,0:T(8,128)} collective-permute-done((f32[512,512]{1,0:T(8,128)S(1)}, f32[512,512]{1,0:T(8,128)}, u32[]{:S(2)}, u32[]{:S(2)}) %collective-permute-start.7) | collective-permute-done | bytes 1048608 | tf_op jit(solution)/shard_map/ppermute | solution.py:19
  848.1 39.9 %custom-call.80 = f32[4,128,128]{1,2,0:T(8,128)} custom-call(f32[4,128,128]{2,1,0:T(8,128)S(1)} %get-tuple-element.169), custom_call_target="InvertDiagBlocksLowerTriangular" | custom-call | tf_op jit(solution)/shard_map/jit(_solve_triangular)/triangular_solve | solution.py:96
  916.3 15.4 all_gather.38
  958.2 21.7 collective-permute-done.11
  1002.1 14.7 scatter_fusion.8
  1016.8 15.2 all_gather.39
  1056.2 21.6 collective-permute-done.14
  1195.0 39.9 %custom-call.84 = f32[4,128,128]{1,2,0:T(8,128)} custom-call(f32[4,128,128]{2,1,0:T(8,128)S(1)} %get-tuple-element.170), custom_call_target="InvertDiagBlocksLowerTriangular" | custom-call | tf_op jit(solution)/shard_map/jit(_solve_triangular)/triangular_solve | solution.py:96
  1261.2 16.2 all_gather.40
  1311.0 45.0 %collective-permute-done.19 = f32[512,512]{1,0:T(8,128)} collective-permute-done((f32[512,512]{1,0:T(8,128)}, f32[512,512]{1,0:T(8,128)}, u32[]{:S(2)}, u32[]{:S(2)}) %collective-permute-start.19) | collective-permute-done | bytes 1048608 | tf_op jit(solution)/shard_map/ppermute | solution.py:19
  1428.4 45.2 %collective-permute-done.23 = f32[512,512]{1,0:T(8,128)} collective-permute-done((f32[512,512]{1,0:T(8,128)S(1)}, f32[512,512]{1,0:T(8,128)}, u32[]{:S(2)}, u32[]{:S(2)}) %collective-permute-start.23) | collective-permute-done | bytes 1048608 | tf_op jit(solution)/shard_map/ppermute | solution.py:19
  1590.9 39.9 %custom-call.88 = f32[4,128,128]{1,2,0:T(8,128)} custom-call(f32[4,128,128]{2,1,0:T(8,128)S(1)} %get-tuple-element.171), custom_call_target="InvertDiagBlocksLowerTriangular" | custom-call | tf_op jit(solution)/shard_map/jit(_solve_triangular)/triangular_solve | solution.py:96
  1656.3 15.2 all-gather
  1692.0 22.5 %collective-permute-done.28 = f32[256,512]{1,0:T(8,128)} collective-permute-done((f32[256,512]{1,0:T(8,128)S(1)}, f32[256,512]{1,0:T(8,128)}, u32[]{:S(2)}, u32[]{:S(2)}) %collective-permute-start.28) | collective-permute-done | bytes 524320 | tf_op jit(solution)/shard_map/ppermute | solution.py:19
  1718.9 47.7 %collective-permute-done.29 = f32[512,512]{1,0:T(8,128)} collective-permute-done((f32[512,512]{1,0:T(8,128)}, f32[512,512]{1,0:T(8,128)}, u32[]{:S(2)}, u32[]{:S(2)}) %collective-permute-start.29) | collective-permute-done | bytes 1048608 | tf_op jit(solution)/shard_map/ppermute | solution.py:19
  1797.3 24.8 %scatter_fusion.5 = f32[4,1024]{1,0:T(4,128)S(1)} fusion(f32[4,1024]{1,0:T(4,128)S(1)} %add.627, s32[512]{0:T(512)S(1)} %fusion.262, f32[512]{0:T(512)S(1)} %bitcast.530), kind=kCustom, calls=%fused_computation.42 | custom fusion | flops 512 | bytes 10240 | tf_op jit(solution)/shard_map/scatter-add | solution.py:147
  1857.4 18.8 collective-permute-done.33
  1909.4 20.8 collective-permute-done.34
  2035.7 39.3 %custom-call.92 = f32[4,128,128]{1,2,0:T(8,128)S(1)} custom-call(f32[4,128,128]{2,1,0:T(8,128)S(1)} %get-tuple-element.172), custom_call_target="InvertDiagBlocksLowerTriangular" | custom-call | tf_op jit(solution)/shard_map/jit(_solve_triangular)/triangular_solve | solution.py:96
  2103.4 61.8 %psum.15 = f32[]{:T(128)} all-reduce(f32[]{:T(128)} %psum.14), channel_id=1, replica_groups=mesh['leaf'=32,'front'=8] {'leaf'}, use_global_device_ids=true, to_apply=%region_60.73 | all-reduce | flops 1 | bytes 8 | tf_op jit(solution)/shard_map/psum | solution.py:155
  (828 shorter events, 1276.9 us)
Async XLA Ops:
  7.2 35.2 %all-gather.6.cloned.1.call-start = ((), (), s32[]{:S(2)}) async-start(), calls=%async_computation | async-start | bytes 2359296 | tf_op jit(solution)/shard_map/all_gather | solution.py:42
  9.2 226.9 %all-gather.8.cloned.1.call-start = ((), (), s32[]{:S(2)}) async-start(), calls=%async_computation.1 | async-start | bytes 1179648 | tf_op jit(solution)/shard_map/all_gather | solution.py:44
  201.2 8.7 collective-permute-start
  210.6 149.7 %all-gather.10.cloned.1.call-start = ((), (), s32[]{:S(2)}) async-start(), calls=%async_computation.2 | async-start | bytes 1179648 | tf_op jit(solution)/shard_map/all_gather | solution.py:42
  236.1 24.7 %collective-permute-start.1 = (f32[512,512]{1,0:T(8,128)}, f32[512,512]{1,0:T(8,128)S(1)}, u32[]{:S(2)}, u32[]{:S(2)}) collective-permute-start(f32[512,512]{1,0:T(8,128)} %all-gather.8.cloned.1.call-done), channel_id=1, source_target_pairs={{0,8},{8,0},{16,24},{24,16},{32,40},{40,32},{48,56},{56,48},{64,72... | collective-permute-start | bytes 3145736 | tf_op jit(solution)/shard_map/ppermute | solution.py:19
  360.3 24.7 %collective-permute-start.2 = (f32[512,512]{1,0:T(8,128)}, f32[512,512]{1,0:T(8,128)S(1)}, u32[]{:S(2)}, u32[]{:S(2)}) collective-permute-start(f32[512,512]{1,0:T(8,128)} %all-gather.10.cloned.1.call-done), channel_id=1, source_target_pairs={{0,8},{8,0},{16,24},{24,16},{32,40},{40,32},{48,56},{56,48},{64,72... | collective-permute-start | bytes 3145736 | tf_op jit(solution)/shard_map/ppermute | solution.py:19
  557.7 6.8 collective-permute-start.3
  579.3 14.0 collective-permute-start.4
  594.5 27.7 %collective-permute-start.5 = (f32[512,512]{1,0:T(8,128)}, f32[512,512]{1,0:T(8,128)}, u32[]{:S(2)}, u32[]{:S(2)}) collective-permute-start(f32[512,512]{1,0:T(8,128)} %pad_maximum_fusion.7), channel_id=1, source_target_pairs={{0,16},{16,0},{8,24},{24,8},{32,48},{48,32},{40,56},{56,40},{64,80... | collective-permute-start | bytes 3145736 | tf_op jit(solution)/shard_map/ppermute | solution.py:19
  687.6 13.4 collective-permute-start.6
  702.1 25.3 %collective-permute-start.7 = (f32[512,512]{1,0:T(8,128)S(1)}, f32[512,512]{1,0:T(8,128)}, u32[]{:S(2)}, u32[]{:S(2)}) collective-permute-start(f32[512,512]{1,0:T(8,128)S(1)} %pad_maximum_fusion.8), channel_id=1, source_target_pairs={{0,16},{16,0},{8,24},{24,8},{32,48},{48,32},{40,56},{56,40},{64,80... | collective-permute-start | bytes 3145736 | tf_op jit(solution)/shard_map/ppermute | solution.py:19
  908.2 8.1 collective-permute-start.8
  931.7 7.8 collective-permute-start.9
  939.6 15.5 collective-permute-start.10
  956.3 23.6 %collective-permute-start.11 = (f32[512,512]{1,0:T(8,128)}, f32[512,512]{1,0:T(8,128)}, u32[]{:S(2)}, u32[]{:S(2)}) collective-permute-start(f32[512,512]{1,0:T(8,128)} %pad_maximum_fusion.10), channel_id=1, source_target_pairs={{0,32},{32,0},{8,40},{40,8},{16,48},{48,16},{24,56},{56,24},{64,96... | collective-permute-start | bytes 3145736 | tf_op jit(solution)/shard_map/ppermute | solution.py:19
  1032.0 7.8 collective-permute-start.12
  1039.8 14.0 collective-permute-start.13
  1055.0 22.9 %collective-permute-start.14 = (f32[512,512]{1,0:T(8,128)S(1)}, f32[512,512]{1,0:T(8,128)}, u32[]{:S(2)}, u32[]{:S(2)}) collective-permute-start(f32[512,512]{1,0:T(8,128)S(1)} %pad_maximum_fusion.11), channel_id=1, source_target_pairs={{0,32},{32,0},{8,40},{40,8},{16,48},{48,16},{24,56},{56,24},{64,96... | collective-permute-start | bytes 3145736 | tf_op jit(solution)/shard_map/ppermute | solution.py:19
  1255.1 6.1 collective-permute-start.15
  1282.5 8.4 collective-permute-start.17
  1291.0 12.2 collective-permute-start.18
  1304.3 51.7 %collective-permute-start.19 = (f32[512,512]{1,0:T(8,128)}, f32[512,512]{1,0:T(8,128)}, u32[]{:S(2)}, u32[]{:S(2)}) collective-permute-start(f32[512,512]{1,0:T(8,128)} %pad_maximum_fusion.13), channel_id=1, source_target_pairs={{0,64},{64,0},{8,72},{72,8},{16,80},{80,16},{24,88},{88,24},{32,96... | collective-permute-start | bytes 3145736 | tf_op jit(solution)/shard_map/ppermute | solution.py:19
  1404.8 8.4 collective-permute-start.21
  1413.3 11.6 collective-permute-start.22
  1426.0 47.6 %collective-permute-start.23 = (f32[512,512]{1,0:T(8,128)S(1)}, f32[512,512]{1,0:T(8,128)}, u32[]{:S(2)}, u32[]{:S(2)}) collective-permute-start(f32[512,512]{1,0:T(8,128)S(1)} %pad_maximum_fusion.14), channel_id=1, source_target_pairs={{0,64},{64,0},{8,72},{72,8},{16,80},{80,16},{24,88},{88,24},{32,96... | collective-permute-start | bytes 3145736 | tf_op jit(solution)/shard_map/ppermute | solution.py:19
  1675.1 5.4 collective-permute-start.26
  1680.6 7.2 collective-permute-start.27
  1687.9 26.7 %collective-permute-start.28 = (f32[256,512]{1,0:T(8,128)S(1)}, f32[256,512]{1,0:T(8,128)}, u32[]{:S(2)}, u32[]{:S(2)}) collective-permute-start(f32[256,512]{1,0:T(8,128)S(1)} %pad_maximum_fusion.22), channel_id=1, source_target_pairs={{0,64},{64,0},{8,72},{72,8},{16,80},{80,16},{24,88},{88,24},{32,96... | collective-permute-start | bytes 1572872 | tf_op jit(solution)/shard_map/ppermute | solution.py:19
  1716.9 49.7 %collective-permute-start.29 = (f32[512,512]{1,0:T(8,128)}, f32[512,512]{1,0:T(8,128)}, u32[]{:S(2)}, u32[]{:S(2)}) collective-permute-start(f32[512,512]{1,0:T(8,128)} %pad_maximum_fusion.16), channel_id=1, source_target_pairs={{0,128},{128,0},{8,136},{136,8},{16,144},{144,16},{24,152},{152,24... | collective-permute-start | bytes 3145736 | tf_op jit(solution)/shard_map/ppermute | solution.py:19
  1844.9 5.7 collective-permute-start.32
  1850.7 25.5 %collective-permute-start.33 = (f32[256,512]{1,0:T(8,128)S(1)}, f32[256,512]{1,0:T(8,128)}, u32[]{:S(2)}, u32[]{:S(2)}) collective-permute-start(f32[256,512]{1,0:T(8,128)S(1)} %pad_maximum_fusion.23), channel_id=1, source_target_pairs={{0,64},{64,0},{8,72},{72,8},{16,80},{80,16},{24,88},{88,24},{32,96... | collective-permute-start | bytes 1572872 | tf_op jit(solution)/shard_map/ppermute | solution.py:19
  1878.6 51.6 %collective-permute-start.34 = (f32[512,512]{1,0:T(8,128)}, f32[512,512]{1,0:T(8,128)}, u32[]{:S(2)}, u32[]{:S(2)}) collective-permute-start(f32[512,512]{1,0:T(8,128)} %pad_maximum_fusion.17), channel_id=1, source_target_pairs={{0,128},{128,0},{8,136},{136,8},{16,144},{144,16},{24,152},{152,24... | collective-permute-start | bytes 3145736 | tf_op jit(solution)/shard_map/ppermute | solution.py:19
  (84 other events, 1350.4 us)
Sparse Core Ops, SparseCore 0:
  10.4 31.8 all-gather.5
  210.7 25.3 all-gather.7
  333.7 26.5 all-gather.9
